TPU v7x, 256 devices: a whole 4x4x8 slice. The times are simulated.
256 devices in a mesh: blk: 64 (over z, y, core), fld: 4 (over x).
Axes of the slice: x: 4, y: 4, z: 8, core: 2. Of those that a mesh axis runs over, the one named last changes fastest.
Arguments:
- first_noise: bfloat16 [256, 131072], P('fld', 'blk'), may hold values from -6 to 6
- second_noise: bfloat16 [256, 131072], P('fld', 'blk'), may hold values from -6 to 6
- first_root: bfloat16 [512, 256, 256], P('blk'), may hold values from -0.375 to 0.375
- second_root: bfloat16 [512, 256, 256], P('blk'), may hold values from -0.375 to 0.375
- cond_weight: bfloat16 [512, 16, 256, 256], P('blk'), may hold values from -0.09375 to 0.09375
- cond_ids: int32 [512, 16], P('blk'), may hold values from 0 to 511, as said below
- krig_weight: bfloat16 [256, 16, 256, 512], P('blk', None, None, 'fld'), may hold values from -0.09375 to 0.09375
- stencil: int32 [256, 16], P('blk'), may hold values from 0 to 1023, as said below
Outputs:
- first_fields: bfloat16 [256, 131072], P('fld', 'blk')
- second_fields: bfloat16 [256, 131072], P('fld', 'blk')
- field_map: float32 [256, 256, 512], P(None, 'blk', 'fld')
Inputs may be any that keep to these rules, and one draw needn't show every extreme that they name: `cond_ids`: ids i with the same i // 8 form the first-level blocks of one index of blk. Among the 128 ids held by one index of blk, at most 4 name blocks of any one index, and exactly 4 name blocks of some index. `stencil`: blocks of index d of blk are ids d * 8 to (d + 1) * 8 - 1 and 512 + d * 8 to 512 + (d + 1) * 8 - 1. Among the 64 ids held by one index of blk, at most 2 name blocks of any one index, and exactly 2 name blocks of some index.
All inputs are finite; a program needn't handle non-finite values.
Results may differ from a plain program's by a relative error of at most 0.0041.
Values may be sent and summed in bfloat16 or wider, within the bound.
A program may use at most 128 MiB of HBM per device.

v0:
```python
import functools

import jax
import jax.numpy as jnp
from jax import lax
from jax.experimental import pallas as pl
from jax.experimental.pallas import tpu as pltpu
from jax.sharding import PartitionSpec as P

MESH = pl.DeviceIdType.MESH
NZ, NY, NC, NX = 8, 4, 2, 4
NB = 8
ROWS = 64
UNIT = 16
PARTS = ((2, 7, ((0, 4), (4, 3))), (2, 6, ((0, 3), (3, 3))))
CUTS = 2
LAG = 10
W = 256
COND = 16
STEN = 16
WHOLE = 2
HALVED = 2
TILES = WHOLE + HALVED
CELLS = 128
NB1 = 512
K = STEN * W


def f32dot(a, b):
    return jnp.dot(a, b, preferred_element_type=jnp.float32)


GROUPS = ((0, 1), (1, 2), (6, 2), (3, 3))


def gather_labels():
    labels = []
    for d in (1, -1):
        labels += [("zB", s, d) for s in (1, 2, 3, 4)]
        labels += [("yA", s, d) for s in (1, 2)]
        labels += [("yB", g, s, d) for g in range(len(GROUPS)) for s in (1, 2)]
        labels += [("zA", s, d, l) for s in (1, 2, 3, 4) for l in range(CUTS)]
    labels += [("DA", g) for g in range(len(GROUPS))]
    labels += [("DB", g, None) for g in range(len(GROUPS) - 1)]
    labels += [("DB", len(GROUPS) - 1, y) for y in range(NY)]
    return {label: i for i, label in enumerate(labels)}


LABELS = gather_labels()


class Gather:
    def __init__(self, buf, send, recv, targets, part):
        self.buf, self.send, self.recv, self.targets = buf, send, recv, targets
        self.per, self.a, self.cuts = part
        self.started = []

    def units(self, core, lo, n, half=0):
        if half:
            cut = (n + (lo % 2 == 0)) // 2
            lo, n = (lo, cut) if half == 1 else (lo + cut, n - cut)
        return pl.ds(core * (NB * self.per) + lo, n)

    def place(self, label, there):
        kind, s, d = label[0], label[-2], label[-1]
        part_a, part_b = (0, self.a), (self.a, NB * self.per - self.a)
        if kind == "zB":
            return self.buf.at[-(s - 1 + there) * d % NZ, 0, self.units(0, *part_b, d if s == 4 else 0)]
        if kind == "zA":
            s, d, l = label[1:]
            units = self.units(0, *self.cuts[l], d if s == 4 else 0)
            return self.buf.at[-(s - 1 + there) * d % NZ, :, units]
        if kind == "yA":
            return self.buf.at[0, -(s - 1 + there) * d % NY, self.units(0, *part_a, d if s == 2 else 0)]
        columns = pl.ds(*GROUPS[label[1]])
        if kind == "yB":
            return self.buf.at[columns, -(s - 1 + there) * d % NY, self.units(0, *part_b, d if s == 2 else 0)]
        if kind == "DA":
            return self.buf.at[columns, :, self.units(there, *part_a)]
        return self.buf.at[columns, slice(None) if d is None else d, self.units(there, *part_b)]

    def copy(self, label):
        i = LABELS[label]
        kind = label[0]
        way = kind[0] if kind[0] == "D" else (kind[0], label[2] if kind == "zA" else label[-1])
        return pltpu.make_async_remote_copy(
            self.place(label, 0), self.place(label, 1), self.send.at[i], self.recv.at[i],
            device_id=self.targets[way], device_id_type=MESH,
        )

    def start(self, *labels):
        for label in labels:
            cp = self.copy(label)
            cp.start()
            self.started.append(cp)

    def wait(self, *labels):
        for label in labels:
            self.copy(label).wait_recv()

    def begin(self):
        self.start(("yA", 1, 1), ("zB", 1, 1), ("yA", 1, -1), ("zB", 1, -1), ("yB", 0, 1, 1), ("yB", 0, 1, -1))

    def z_b(self, s):
        for d in (1, -1):
            self.wait(("zB", s, d))
            if s < 4:
                self.start(("zB", s + 1, d))
            if s == 2:
                g = 2 if d == 1 else 1
                self.start(("yB", g, 1, 1), ("yB", g, 1, -1))
        if s == 4:
            self.start(("yB", 3, 1, 1), ("yB", 3, 1, -1), ("DB", 3, 0))

    def z_a(self, s):
        for l in range(CUTS):
            for d in (1, -1):
                self.wait(("zA", s, d, l))
                if s < 4:
                    self.start(("zA", s + 1, d, l))
        if s == 2:
            self.start(("DA", 1), ("DA", 2))
        if s == 4:
            self.start(("DA", 3))

    def y_a(self):
        for d in (1, -1):
            self.wait(("yA", 1, d))
            self.start(("yA", 2, d))

    def y_a_end(self):
        self.wait(("yA", 2, 1), ("yA", 2, -1))
        for l in range(CUTS):
            self.start(("zA", 1, 1, l), ("zA", 1, -1, l))
        self.start(("DA", 0))

    def y_b(self, *groups):
        for g in groups:
            for d in (1, -1):
                self.wait(("yB", g, 1, d))
                self.start(("yB", g, 2, d))
                if g == 3:
                    self.start(("DB", 3, -d % NY))

    def y_b_end(self, *groups):
        for g in groups:
            self.wait(("yB", g, 2, 1), ("yB", g, 2, -1))
            self.start(("DB", g, 2 if g == 3 else None))

    def steps(self):
        return [
            lambda: self.y_a(),
            lambda: self.z_b(1),
            lambda: self.y_a_end(),
            lambda: self.y_b(0),
            lambda: self.z_b(2),
            lambda: self.z_b(3),
            lambda: self.z_a(1),
            lambda: self.y_b(1, 2),
            lambda: self.z_b(4),
            lambda: self.y_b_end(0),
            lambda: self.z_a(2),
            lambda: self.y_b_end(1, 2),
            lambda: self.z_a(3),
            lambda: self.y_b(3),
            lambda: self.z_a(4),
            lambda: self.y_b_end(3),
        ]

    def run(self, between={}):
        for i, step in enumerate(self.steps()):
            step()
            for work in between.get(i, ()):
                work()

    def arrive(self):
        for label in LABELS:
            if label[0] in ("DA", "DB"):
                self.wait(label)

    def finish(self):
        for cp in self.started:
            cp.wait_send()
        self.started = []


def kernel(
    noise1_hbm, noise2_hbm, root1_hbm, root2_hbm, cond_hbm, cond_ids, krig_hbm, stencil,
    out1, out2, out_map, krig_in,
    weights, noise, roots, fields1, fields2, whole, mine, theirs, field_map, away_whole, away_halved,
    local, krig_send, krig_recv, x_send, x_recv, map_send, map_recv, *by_part,
):
    parts = range(len(PARTS))
    g1, g2, picked, g1_send, g1_recv, g2_send, g2_recv = (
        by_part[len(PARTS) * i : len(PARTS) * (i + 1)] for i in range(7)
    )
    blk, x = lax.axis_index("blk"), lax.axis_index("fld")
    z, y, c = blk // (NY * NC), lax.rem(blk // NC, NY), lax.rem(blk, NC)
    near, far = x + 1 - 2 * lax.rem(x, 2), NX - 1 - x

    def device(dz, dy, dc):
        zz, yy, cc = lax.rem(z + dz + NZ, NZ), lax.rem(y + dy + NY, NY), lax.rem(c + dc, NC)
        return ((zz * NY + yy) * NC + cc, x)

    targets = {("z", d): device(d, 0, 0) for d in (1, -1)}
    targets |= {("y", d): device(0, d, 0) for d in (1, -1)}
    targets["D"] = device(0, 0, 1)
    first = [Gather(g1[p], g1_send[p], g1_recv[p], targets, PARTS[p]) for p in parts]
    second = [Gather(g2[p], g2_send[p], g2_recv[p], targets, PARTS[p]) for p in parts]

    def along(r):
        return (blk, lax.rem(x + r + NX, NX))

    barrier = pltpu.get_barrier_semaphore()
    for to in [*targets.values(), along(1), along(2), along(3)]:
        pl.semaphore_signal(barrier, inc=1, device_id=to, device_id_type=MESH)

    counter = iter(range(100))

    def load(src, dst):
        cp = pltpu.make_async_copy(src, dst, local.at[next(counter)])
        cp.start()
        return cp

    loads = [load(noise1_hbm, noise.at[0]), load(root1_hbm, roots.at[0])]
    for cp in loads:
        cp.wait()

    def sites(b):
        return pl.ds(pl.multiple_of(b * W, W), W)

    def rows_of(p):
        return UNIT * sum(part[0] for part in PARTS[:p]), UNIT * PARTS[p][0]

    def block_of(g, p, i):
        kz, ky = ((i >> 6) - z) & (NZ - 1), ((i >> 4) - y) & (NY - 1)
        per = PARTS[p][0]
        at = pl.ds(((((i >> 3) - c) & 1) * NB + (i & (NB - 1))) * per, per)
        return g[p][kz, ky, at].reshape(per * UNIT, W)

    def put(g, out, p, b, block):
        per = PARTS[p][0]
        lo, n = rows_of(p)
        g[p][0, 0, pl.ds(b * per, per)] = block.reshape(per, UNIT, W)
        out[lo : lo + n, sites(b)] = block

    @pl.loop(0, NB)
    def _(b):
        block = f32dot(noise[0, :, sites(b)], roots[0, b]).astype(jnp.bfloat16)
        for p in parts:
            lo, n = rows_of(p)
            put(g1, fields1, p, b, block[lo : lo + n])

    pl.semaphore_wait(barrier, 8)
    first[0].begin()

    def krig_copy(i, src, dst, to):
        return pltpu.make_async_remote_copy(
            src, dst, krig_send.at[i], krig_recv.at[i], device_id=to, device_id_type=MESH
        )

    def whole_copy(t, r):
        return krig_copy(3 * t + r - 1, krig_hbm.at[t], krig_in.at[3 * t + r - 1], along(-r))

    def passed_copy(t, d):
        half = pl.ds(0 if d == 1 else K // 2, K // 2)
        src, dst = krig_in.at[3 * t + (2 if d == 1 else 0), half], krig_in.at[3 * t + 1, half]
        return krig_copy(3 * t + 1 if d == 1 else 3 * WHOLE + HALVED + t, src, dst, along(d))

    def halved_copy(t):
        i = 3 * WHOLE + t
        return krig_copy(i, krig_hbm.at[WHOLE + t], krig_in.at[i], (blk, near if t == 0 else far))

    krig_sends = [whole_copy(t, r) for t in range(WHOLE) for r in (3, 1)] + [halved_copy(t) for t in range(HALVED)]
    for cp in krig_sends:
        cp.start()
    noise2_load, root2_load = load(noise2_hbm, noise.at[1]), load(root2_hbm, roots.at[1])
    cond_loads = [load(cond_hbm.at[b], weights.at[b]) for b in range(NB)]
    out_copies = [load(fields1, out1)]

    def pass_weights():
        for t in range(WHOLE):
            for r, d in ((3, 1), (1, -1)):
                whole_copy(t, r).wait_recv()
                cp = passed_copy(t, d)
                cp.start()
                krig_sends.append(cp)

    def second_block(p, b):
        lo, n = rows_of(p)
        for k in range(COND):
            picked[p][:, k * W : (k + 1) * W] = block_of(g1, p, cond_ids[b, k])
        total = f32dot(picked[p][...], weights[b]) + f32dot(noise[1, lo : lo + n, sites(b)], roots[1, b])
        put(g2, fields2, p, b, total.astype(jnp.bfloat16))

    def second_blocks(p, lo, hi):
        return lambda: pl.loop(lo, hi)(lambda b: second_block(p, b))

    def cells(r):
        return pl.ds(CELLS * (r % 2), CELLS)

    whole_loads, halved_loads = [[] for _ in range(WHOLE)], [[] for _ in range(HALVED)]

    def load_whole():
        for t in range(WHOLE):
            whole_loads[t].append(load(krig_hbm.at[t], weights.at[2 * t, :, cells(0)]))
            for r in (1, 3):
                whole_loads[t].append(load(krig_in.at[3 * t + r - 1], weights.at[2 * t + r // 2, :, cells(r)]))

    def load_halved():
        for t in range(HALVED):
            halved_copy(t).wait_recv()
            halved_loads[t].append(load(krig_hbm.at[WHOLE + t], weights.at[2 * WHOLE + t, :, cells(0)]))
            halved_loads[t].append(load(krig_in.at[3 * WHOLE + t], weights.at[2 * WHOLE + t, :, cells(1)]))

    def load_passed():
        for t in range(WHOLE):
            for d in (1, -1):
                passed_copy(t, d).wait_recv()
            whole_loads[t].append(load(krig_in.at[3 * t + 1], weights.at[2 * t + 1, :, cells(2)]))

    def pick(p, t, into):
        lo, n = rows_of(p)
        for s in range(STEN):
            i = stencil[t, s]
            one = block_of(g1, p, jnp.minimum(i, NB1 - 1))
            two = block_of(g2, p, jnp.maximum(i - NB1, 0))
            into[lo : lo + n, s * W : (s + 1) * W] = jnp.where(i < NB1, one, two)

    def field_copy(p, t):
        rows = pl.ds(*rows_of(p))
        i = HALVED * p + t
        return pltpu.make_async_remote_copy(
            mine.at[t, rows], theirs.at[t, rows], x_send.at[i], x_recv.at[i],
            device_id=(blk, far if t == 0 else near), device_id_type=MESH,
        )

    sends = []

    def send(cp):
        cp.start()
        sends.append(cp)

    def exchange(p, t):
        pick(p, WHOLE + t, mine.at[t])
        send(field_copy(p, t))

    todo = []
    for i, gather in enumerate(first + second):
        steps = [gather.begin] + gather.steps() + [gather.arrive]
        todo += [(LAG * i + k, step) for k, step in enumerate(steps)][1 if i == 0 else 0 :]
    todo += [(17.1, cp.wait) for cp in [noise2_load, root2_load] + cond_loads]
    for p in parts:
        at = LAG * p + 17.2
        todo += [(at + w, second_blocks(p, lo, lo + 2)) for w, lo in ((0, 0), (1, 2), (2, 4), (2.5, 6))]
    todo += [(25.5, pass_weights), (30.5, load_whole), (30.6, lambda: out_copies.append(load(fields2, out2)))]
    todo += [(33.5, first[0].finish), (34.5, first[1].finish)]
    todo += [(37.2, lambda: exchange(0, 0)), (37.3, lambda: exchange(0, 1))]
    todo += [(39.2 + t, functools.partial(pick, 0, t, whole.at[t])) for t in range(WHOLE)]
    todo += [(41.5, load_halved), (42.5, second[0].finish)]
    for _, work in sorted(todo, key=lambda entry: entry[0]):
        work()

    for t in range(HALVED):
        exchange(1, t)
    load_passed()
    second[1].finish()

    def fields_of(device):
        return pl.ds(pl.multiple_of(device * ROWS, ROWS), ROWS)

    def map_copy(i, src, t, device, to):
        return pltpu.make_async_remote_copy(
            src, field_map.at[t, fields_of(device)], map_send.at[i], map_recv.at[i], device_id=to, device_id_type=MESH
        )

    for t in range(WHOLE):
        pick(1, t, whole.at[t])
        for cp in whole_loads[t]:
            cp.wait()
        for h in range(2):
            total = f32dot(whole[t], weights[2 * t + h])
            for r in (2 * h, 2 * h + 1):
                part = total[:, (r % 2) * CELLS : (r % 2 + 1) * CELLS]
                if r == 0:
                    field_map[t, fields_of(x), :] = part
                else:
                    away_whole[t, r - 1] = part
                    send(map_copy(3 * t + r - 1, away_whole.at[t, r - 1], t, x, along(r)))
    for h in range(2):
        for t in range(HALVED):
            if h == 0:
                for cp in halved_loads[t]:
                    cp.wait()
            else:
                for p in parts:
                    field_copy(p, t).wait_recv()
            total = f32dot((theirs if h else mine)[t], weights[2 * WHOLE + t])
            whose = (far if t == 0 else near) if h else x
            field_map[WHOLE + t, fields_of(whose), :] = total[:, :CELLS]
            away_halved[t, h] = total[:, CELLS:]
            send(map_copy(3 * WHOLE + 2 * t + h, away_halved.at[t, h], WHOLE + t, whose, (blk, near if t == 0 else far)))
    for t in range(WHOLE):
        for r in range(1, NX):
            map_copy(3 * t + r - 1, away_whole.at[t, r - 1], t, lax.rem(x - r + NX, NX), along(r)).wait_recv()
        out_copies.append(load(field_map.at[t], out_map.at[t]))
    for t in range(HALVED):
        for h in range(2):
            mate = near if t == 0 else far
            device = mate if h == 0 else (NX - 1 - mate if t == 0 else mate + 1 - 2 * lax.rem(mate, 2))
            map_copy(3 * WHOLE + 2 * t + h, away_halved.at[t, h], WHOLE + t, device, (blk, mate)).wait_recv()
        out_copies.append(load(field_map.at[WHOLE + t], out_map.at[WHOLE + t]))
    for cp in krig_sends + sends:
        cp.wait_send()
    for cp in out_copies:
        cp.wait()


def hand_out(first_in, second_in, map_in, first_out, second_out, map_out):
    first_out[...] = first_in[...]
    second_out[...] = second_in[...]
    for t in range(TILES):
        map_out[:, t, :] = map_in[t]


def on_device(
    first_noise, second_noise, first_root, second_root, cond_weight, cond_ids, krig_weight, stencil
):
    bf16, f32 = jnp.bfloat16, jnp.float32
    hbm, smem = (pl.BlockSpec(memory_space=m) for m in (pl.ANY, pltpu.SMEM))
    n = len(LABELS)
    dma = pltpu.SemaphoreType.DMA
    fields = jax.ShapeDtypeStruct((ROWS, NB * W), bf16)
    by_part = [pltpu.VMEM((NZ, NY, NC * NB * p[0], UNIT, W), bf16) for p in PARTS] * 2
    by_part += [pltpu.VMEM((p[0] * UNIT, COND * W), bf16) for p in PARTS]
    by_part += [dma((n,))] * (4 * len(PARTS))
    first_fields, second_fields, tiles, _ = pl.pallas_call(
        kernel,
        out_shape=(
            fields,
            fields,
            jax.ShapeDtypeStruct((TILES, NX * ROWS, CELLS), f32),
            jax.ShapeDtypeStruct((3 * WHOLE + HALVED, K, CELLS), bf16),
        ),
        in_specs=[hbm, hbm, hbm, hbm, hbm, smem, hbm, smem],
        out_specs=(hbm, hbm, hbm, hbm),
        scratch_shapes=[
            pltpu.VMEM((NB, COND * W, W), bf16),
            pltpu.VMEM((2, ROWS, NB * W), bf16),
            pltpu.VMEM((2, NB, W, W), bf16),
            pltpu.VMEM((ROWS, NB * W), bf16),
            pltpu.VMEM((ROWS, NB * W), bf16),
            pltpu.VMEM((WHOLE, ROWS, K), bf16),
            pltpu.VMEM((HALVED, ROWS, K), bf16),
            pltpu.VMEM((HALVED, ROWS, K), bf16),
            pltpu.VMEM((TILES, NX * ROWS, CELLS), f32),
            pltpu.VMEM((WHOLE, NX - 1, ROWS, CELLS), f32),
            pltpu.VMEM((HALVED, 2, ROWS, CELLS), f32),
            dma((40,)),
            dma((4 * WHOLE + HALVED,)), dma((4 * WHOLE + HALVED,)),
            dma((HALVED * len(PARTS),)), dma((HALVED * len(PARTS),)),
            dma((3 * WHOLE + 2 * HALVED,)), dma((3 * WHOLE + 2 * HALVED,)),
            *by_part,
        ],
        compiler_params=pltpu.CompilerParams(
            collective_id=0, has_side_effects=True, vmem_limit_bytes=60 << 20
        ),
        cost_estimate=pl.CostEstimate(flops=2300000000, bytes_accessed=30000000, transcendentals=0),
    )(
        first_noise, second_noise, first_root, second_root,
        cond_weight.reshape(NB, COND * W, W), cond_ids,
        krig_weight.reshape(TILES, K, CELLS), stencil,
    )
    vmem = pl.BlockSpec(memory_space=pltpu.VMEM)
    return pl.pallas_call(
        hand_out,
        out_shape=(fields, fields, jax.ShapeDtypeStruct((NX * ROWS, TILES, CELLS), f32)),
        in_specs=[vmem, vmem, vmem],
        out_specs=(vmem, vmem, vmem),
    )(first_fields, second_fields, tiles)


def solution(mesh):
    placed = (
        P("fld", "blk"),
        P("fld", "blk"),
        P("blk", None, None),
        P("blk", None, None),
        P("blk", None, None, None),
        P("blk", None),
        P("blk", None, None, "fld"),
        P("blk", None),
    )
    return jax.shard_map(
        on_device,
        mesh=mesh,
        in_specs=placed,
        out_specs=(P("fld", "blk"), P("fld", "blk"), P(None, "blk", "fld")),
        check_vma=False,
    )
```

profile of v0, /device:TPU:1, one launch (start us, length us, event | category | flops | bytes accessed | tf_op | source)
XLA Modules:
  0.0 137.4 jit_solution(6629076690100492549)
XLA Ops:
  0.6 134.5 %shard_map.103 = (bf16[64,2048]{1,0:T(8,128)(2,1)}, bf16[64,2048]{1,0:T(8,128)(2,1)}, f32[4,256,128]{2,1,0:T(8,128)}, bf16[8,4096,128]{2,1,0:T(8,128)(2,1)}) custom-call(bf16[64,2048]{1,0:T(8,128)(2,1)} %noise1_hbm.1, bf16[64,2048]{1,0:T(8,128)(2,1)} %noise2_hbm.1, bf16[8,256,256]{2,1,0:T(8,128)(2,1)} %root1_hbm.1, bf16[8,256,256]{2,1,0:T(8,128)(2,1)} %root2_hbm.1, ...), custom_call_target="tpu_custom_call" | custom-call | flops 2300000000 | bytes 30000000 | tf_op jit(solution)/shard_map/pallas_call | solution.py:437
  135.1 2.3 %shard_map.104 = (bf16[64,2048]{1,0:T(8,128)(2,1)}, bf16[64,2048]{1,0:T(8,128)(2,1)}, f32[256,4,128]{2,1,0:T(4,128)}) custom-call(bf16[64,2048]{1,0:T(8,128)(2,1)} %get-tuple-element.6.first_in, bf16[64,2048]{1,0:T(8,128)(2,1)} %get-tuple-element.7.second_in, f32[4,256,128]{2,1,0:T(8,128)} %get-tuple-element.8.map_in), custom_call_target="tpu_custom_call" | custom-call | tf_op jit(solution)/shard_map/pallas_call | solution.py:475
where the time goes:
time: 138 us; the launch traced here: 137 us
  Pallas kernels  137 us (99%)
    pallas_call x1, Pallas kernels, on_device(): pl.pallas_call(kernel, out_shape=(fields, fields, jax.ShapeDtypeStruct((T...  134 us

commit v1 on v0

--- a/solution.py
+++ b/solution.py
@@ -14,7 +14,6 @@
 UNIT = 16
 PARTS = ((2, 7, ((0, 4), (4, 3))), (2, 6, ((0, 3), (3, 3))))
 CUTS = 2
-LAG = 10
 W = 256
 COND = 16
 STEN = 16
@@ -30,30 +29,63 @@
     return jnp.dot(a, b, preferred_element_type=jnp.float32)
 
 
-GROUPS = ((0, 1), (1, 2), (6, 2), (3, 3))
-
-
-def gather_labels():
-    labels = []
+COLUMNS = (0, 1, 7, 2, 6, 3, 5, 4)
+LAST = COLUMNS[-1]
+
+
+def gather_steps():
+    steps = [((), (("yA", 1, 1), ("zB", 1, 1), ("yA", 1, -1), ("zB", 1, -1), ("yB", 0, 1, 1), ("yB", 0, 1, -1)))]
     for d in (1, -1):
-        labels += [("zB", s, d) for s in (1, 2, 3, 4)]
-        labels += [("yA", s, d) for s in (1, 2)]
-        labels += [("yB", g, s, d) for g in range(len(GROUPS)) for s in (1, 2)]
-        labels += [("zA", s, d, l) for s in (1, 2, 3, 4) for l in range(CUTS)]
-    labels += [("DA", g) for g in range(len(GROUPS))]
-    labels += [("DB", g, None) for g in range(len(GROUPS) - 1)]
-    labels += [("DB", len(GROUPS) - 1, y) for y in range(NY)]
-    return {label: i for i, label in enumerate(labels)}
-
-
-LABELS = gather_labels()
+        steps += [((("yA", 1, d),), (("yA", 2, d),))]
+        steps += [((("zB", s, d),), (("zB", s + 1, d),) if s < 4 else ()) for s in (1, 2, 3, 4)]
+    cuts = [(d, l) for l in range(CUTS) for d in (1, -1)]
+    steps += [((("yA", 2, 1), ("yA", 2, -1)), tuple(("zA", 1, *cut) for cut in cuts) + (("DA", 0),))]
+
+    def through(kind, column, *rest):
+        ways = ((1, -1),) if column == 4 else ((-1,),) if column < 4 else ((1,),)
+        return tuple((kind, min(column, NZ - column), d, *rest) for way in ways for d in way)
+
+    for o in COLUMNS[1:]:
+        end = (("DB", o, 0),) if o == LAST else ()
+        steps += [(through("zB", o), (("yB", o, 1, 1), ("yB", o, 1, -1)) + end)]
+    for o in COLUMNS:
+        for d in (1, -1):
+            end = (("DB", o, -d % NY),) if o == LAST else ()
+            steps += [((("yB", o, 1, d),), (("yB", o, 2, d),) + end)]
+        steps += [((("yB", o, 2, 1), ("yB", o, 2, -1)), (("DB", o, 2 if o == LAST else None),))]
+    for s in (1, 2, 3, 4):
+        steps += [((("zA", s, *cut),), (("zA", s + 1, *cut),) if s < 4 else ()) for cut in cuts]
+    for o in COLUMNS[1:]:
+        steps += [(sum((through("zA", o, l) for l in range(CUTS)), ()), (("DA", o),))]
+    handed = tuple(label for _, starts in steps for label in starts if label[0] in ("DA", "DB"))
+    return steps + [(handed, ())]
+
+
+STEPS = gather_steps()
+LABELS = {label: i for i, label in enumerate(label for _, starts in STEPS for label in starts)}
+ORDER = (
+    101, 106, 102, 113, 107, 112, 119, 120, 111, 103, 115, 108, 114, 126, 125, 123, 122, 121, 143, 144, 131,
+    132, 145, 160, 146, 159, 128, 129, 127, 104, 117, 109, 116, 124, 133, 130, 147, 148, 137, 138, 200, 149,
+    162, 150, 161, 134, 105, 135, 110, 118, 139, 201, 206, 151, 152, 219, 220, 202, 213, 207, 212, 136, 140,
+    153, 164, 141, 154, 163, 211, 155, 156, 221, 225, 203, 215, 208, 214, 226, 158, 222, 157, 165, 223, 142,
+    244, 243, 166, 231, 232, 0, 1, 246, 259, 245, 260, 2, 228, 229, 209, 216, 3, 204, 217, 227, 224, 4, 248,
+    233, 247, 300, 230, 250, 261, 249, 262, 234, 235, 210, 205, 218, 237, 238, 252, 251, 301, 306, 307, 312,
+    302, 313, 319, 320, 236, 9, 254, 263, 253, 264, 256, 240, 241, 255, 239, 308, 314, 311, 303, 315, 258,
+    257, 265, 323, 322, 309, 316, 326, 325, 321, 343, 242, 344, 266, 328, 329, 345, 360, 5, 346, 359, 331, 6,
+    332, 304, 317, 310, 324, 7, 334, 335, 8, 347, 348, 327, 330, 349, 362, 333, 350, 361, 10, 11, 305, 318,
+    400, 12, 337, 338, 336, 352, 351, 340, 341, 13, 354, 363, 353, 364, 401, 406, 407, 412, 402, 413, 419, 18,
+    420, 339, 356, 355, 342, 358, 411, 357, 365, 408, 414, 422, 423, 366, 403, 415, 14, 425, 426, 15, 444,
+    443, 421, 428, 446, 459, 429, 445, 460, 16, 424, 409, 416, 404, 417, 431, 432, 17, 19, 427, 448, 447, 430,
+    434, 450, 461, 449, 462, 435, 410, 405, 418, 437, 438, 452, 433, 451, 436, 454, 463, 453, 464, 440, 441,
+    456, 455, 439, 457, 458, 465, 442, 466,
+)
 
 
 class Gather:
     def __init__(self, buf, send, recv, targets, part):
         self.buf, self.send, self.recv, self.targets = buf, send, recv, targets
         self.per, self.a, self.cuts = part
-        self.started = []
+        self.started, self.here = [], set()
 
     def units(self, core, lo, n, half=0):
         if half:
@@ -72,12 +104,12 @@
             return self.buf.at[-(s - 1 + there) * d % NZ, :, units]
         if kind == "yA":
             return self.buf.at[0, -(s - 1 + there) * d % NY, self.units(0, *part_a, d if s == 2 else 0)]
-        columns = pl.ds(*GROUPS[label[1]])
+        column = label[1]
         if kind == "yB":
-            return self.buf.at[columns, -(s - 1 + there) * d % NY, self.units(0, *part_b, d if s == 2 else 0)]
+            return self.buf.at[column, -(s - 1 + there) * d % NY, self.units(0, *part_b, d if s == 2 else 0)]
         if kind == "DA":
-            return self.buf.at[columns, :, self.units(there, *part_a)]
-        return self.buf.at[columns, slice(None) if d is None else d, self.units(there, *part_b)]
+            return self.buf.at[column, :, self.units(there, *part_a)]
+        return self.buf.at[column, slice(None) if d is None else d, self.units(there, *part_b)]
 
     def copy(self, label):
         i = LABELS[label]
@@ -88,95 +120,15 @@
             device_id=self.targets[way], device_id_type=MESH,
         )
 
-    def start(self, *labels):
-        for label in labels:
+    def step(self, k):
+        for label in STEPS[k][0]:
+            if label not in self.here:
+                self.here.add(label)
+                self.copy(label).wait_recv()
+        for label in STEPS[k][1]:
             cp = self.copy(label)
             cp.start()
             self.started.append(cp)
-
-    def wait(self, *labels):
-        for label in labels:
-            self.copy(label).wait_recv()
-
-    def begin(self):
-        self.start(("yA", 1, 1), ("zB", 1, 1), ("yA", 1, -1), ("zB", 1, -1), ("yB", 0, 1, 1), ("yB", 0, 1, -1))
-
-    def z_b(self, s):
-        for d in (1, -1):
-            self.wait(("zB", s, d))
-            if s < 4:
-                self.start(("zB", s + 1, d))
-            if s == 2:
-                g = 2 if d == 1 else 1
-                self.start(("yB", g, 1, 1), ("yB", g, 1, -1))
-        if s == 4:
-            self.start(("yB", 3, 1, 1), ("yB", 3, 1, -1), ("DB", 3, 0))
-
-    def z_a(self, s):
-        for l in range(CUTS):
-            for d in (1, -1):
-                self.wait(("zA", s, d, l))
-                if s < 4:
-                    self.start(("zA", s + 1, d, l))
-        if s == 2:
-            self.start(("DA", 1), ("DA", 2))
-        if s == 4:
-            self.start(("DA", 3))
-
-    def y_a(self):
-        for d in (1, -1):
-            self.wait(("yA", 1, d))
-            self.start(("yA", 2, d))
-
-    def y_a_end(self):
-        self.wait(("yA", 2, 1), ("yA", 2, -1))
-        for l in range(CUTS):
-            self.start(("zA", 1, 1, l), ("zA", 1, -1, l))
-        self.start(("DA", 0))
-
-    def y_b(self, *groups):
-        for g in groups:
-            for d in (1, -1):
-                self.wait(("yB", g, 1, d))
-                self.start(("yB", g, 2, d))
-                if g == 3:
-                    self.start(("DB", 3, -d % NY))
-
-    def y_b_end(self, *groups):
-        for g in groups:
-            self.wait(("yB", g, 2, 1), ("yB", g, 2, -1))
-            self.start(("DB", g, 2 if g == 3 else None))
-
-    def steps(self):
-        return [
-            lambda: self.y_a(),
-            lambda: self.z_b(1),
-            lambda: self.y_a_end(),
-            lambda: self.y_b(0),
-            lambda: self.z_b(2),
-            lambda: self.z_b(3),
-            lambda: self.z_a(1),
-            lambda: self.y_b(1, 2),
-            lambda: self.z_b(4),
-            lambda: self.y_b_end(0),
-            lambda: self.z_a(2),
-            lambda: self.y_b_end(1, 2),
-            lambda: self.z_a(3),
-            lambda: self.y_b(3),
-            lambda: self.z_a(4),
-            lambda: self.y_b_end(3),
-        ]
-
-    def run(self, between={}):
-        for i, step in enumerate(self.steps()):
-            step()
-            for work in between.get(i, ()):
-                work()
-
-    def arrive(self):
-        for label in LABELS:
-            if label[0] in ("DA", "DB"):
-                self.wait(label)
 
     def finish(self):
         for cp in self.started:
@@ -252,7 +204,7 @@
             put(g1, fields1, p, b, block[lo : lo + n])
 
     pl.semaphore_wait(barrier, 8)
-    first[0].begin()
+    first[0].step(0)
 
     def krig_copy(i, src, dst, to):
         return pltpu.make_async_remote_copy(
@@ -345,21 +297,23 @@
         pick(p, WHOLE + t, mine.at[t])
         send(field_copy(p, t))
 
-    todo = []
-    for i, gather in enumerate(first + second):
-        steps = [gather.begin] + gather.steps() + [gather.arrive]
-        todo += [(LAG * i + k, step) for k, step in enumerate(steps)][1 if i == 0 else 0 :]
-    todo += [(17.1, cp.wait) for cp in [noise2_load, root2_load] + cond_loads]
-    for p in parts:
-        at = LAG * p + 17.2
-        todo += [(at + w, second_blocks(p, lo, lo + 2)) for w, lo in ((0, 0), (1, 2), (2, 4), (2.5, 6))]
-    todo += [(25.5, pass_weights), (30.5, load_whole), (30.6, lambda: out_copies.append(load(fields2, out2)))]
-    todo += [(33.5, first[0].finish), (34.5, first[1].finish)]
-    todo += [(37.2, lambda: exchange(0, 0)), (37.3, lambda: exchange(0, 1))]
-    todo += [(39.2 + t, functools.partial(pick, 0, t, whole.at[t])) for t in range(WHOLE)]
-    todo += [(41.5, load_halved), (42.5, second[0].finish)]
-    for _, work in sorted(todo, key=lambda entry: entry[0]):
-        work()
+    def wait_cond():
+        for cp in [noise2_load, root2_load] + cond_loads:
+            cp.wait()
+
+    def copy_second():
+        out_copies.append(load(fields2, out2))
+
+    other = [wait_cond] + [second_blocks(p, b, b + 2) for p in parts for b in range(0, NB, 2)]
+    other += [pass_weights, load_whole, copy_second, first[0].finish, first[1].finish]
+    other += [functools.partial(exchange, 0, t) for t in range(HALVED)]
+    other += [functools.partial(pick, 0, t, whole.at[t]) for t in range(WHOLE)]
+    other += [load_halved, second[0].finish]
+    for k in ORDER:
+        if k < 100:
+            other[k]()
+        else:
+            (first + second)[k // 100 - 1].step(k % 100)
 
     for t in range(HALVED):
         exchange(1, t)

time: 138 us -> 133 us (0.964)
  Pallas kernels: 137 us -> 132 us
    pallas_call x1, Pallas kernels: 134 us -> 130 us  [on_device(): pl.pallas_call(kernel, out_shape=(fields, fields, jax.ShapeDtypeStruct((T...]
where the time goes in v1:
time: 133 us
  Pallas kernels  132 us (99%)
    pallas_call x1, Pallas kernels, on_device(): pl.pallas_call(kernel, out_shape=(fields, fields, jax.ShapeDtypeStruct((T...  130 us

profile of v1, /device:TPU:1, one launch (start us, length us, event | category | flops | bytes accessed | tf_op | source)
XLA Modules:
  0.0 132.8 jit_solution(11245197357320963786)
XLA Ops:
  0.6 129.9 %shard_map.103 = (bf16[64,2048]{1,0:T(8,128)(2,1)}, bf16[64,2048]{1,0:T(8,128)(2,1)}, f32[4,256,128]{2,1,0:T(8,128)}, bf16[8,4096,128]{2,1,0:T(8,128)(2,1)}) custom-call(bf16[64,2048]{1,0:T(8,128)(2,1)} %noise1_hbm.1, bf16[64,2048]{1,0:T(8,128)(2,1)} %noise2_hbm.1, bf16[8,256,256]{2,1,0:T(8,128)(2,1)} %root1_hbm.1, bf16[8,256,256]{2,1,0:T(8,128)(2,1)} %root2_hbm.1, ...), custom_call_target="tpu_custom_call" | custom-call | flops 2300000000 | bytes 30000000 | tf_op jit(solution)/shard_map/pallas_call | solution.py:391
  130.5 2.3 %shard_map.104 = (bf16[64,2048]{1,0:T(8,128)(2,1)}, bf16[64,2048]{1,0:T(8,128)(2,1)}, f32[256,4,128]{2,1,0:T(4,128)}) custom-call(bf16[64,2048]{1,0:T(8,128)(2,1)} %get-tuple-element.6.first_in, bf16[64,2048]{1,0:T(8,128)(2,1)} %get-tuple-element.7.second_in, f32[4,256,128]{2,1,0:T(8,128)} %get-tuple-element.8.map_in), custom_call_target="tpu_custom_call" | custom-call | tf_op jit(solution)/shard_map/pallas_call | solution.py:429

commit v2 on v1

--- a/solution.py
+++ b/solution.py
@@ -370,11 +370,25 @@
         cp.wait()
 
 
-def hand_out(first_in, second_in, map_in, first_out, second_out, map_out):
-    first_out[...] = first_in[...]
-    second_out[...] = second_in[...]
-    for t in range(TILES):
-        map_out[:, t, :] = map_in[t]
+def hand_out(first_in, second_in, map_in, first_out, second_out, map_out, held, tiles, turned, sem):
+    def copy(src, dst, i):
+        cp = pltpu.make_async_copy(src, dst, sem.at[i])
+        cp.start()
+        return cp
+
+    tile_in = copy(map_in, tiles, 0)
+    fields_in = [copy(src, held.at[i], 1 + i) for i, src in enumerate((first_in, second_in))]
+    out = []
+    for i, dst in enumerate((first_out, second_out)):
+        if i == 0:
+            tile_in.wait()
+            for t in range(TILES):
+                turned[:, t, :] = tiles[t]
+            out.append(copy(turned, map_out, 3))
+        fields_in[i].wait()
+        out.append(copy(held.at[i], dst, 4 + i))
+    for cp in out:
+        cp.wait()
 
 
 def on_device(
@@ -425,12 +439,18 @@
         cond_weight.reshape(NB, COND * W, W), cond_ids,
         krig_weight.reshape(TILES, K, CELLS), stencil,
     )
-    vmem = pl.BlockSpec(memory_space=pltpu.VMEM)
+    field_map = jax.ShapeDtypeStruct((NX * ROWS, TILES, CELLS), f32)
     return pl.pallas_call(
         hand_out,
-        out_shape=(fields, fields, jax.ShapeDtypeStruct((NX * ROWS, TILES, CELLS), f32)),
-        in_specs=[vmem, vmem, vmem],
-        out_specs=(vmem, vmem, vmem),
+        out_shape=(fields, fields, field_map),
+        in_specs=[hbm, hbm, hbm],
+        out_specs=(hbm, hbm, hbm),
+        scratch_shapes=[
+            pltpu.VMEM((2, ROWS, NB * W), bf16),
+            pltpu.VMEM((TILES, NX * ROWS, CELLS), f32),
+            pltpu.VMEM((NX * ROWS, TILES, CELLS), f32),
+            dma((6,)),
+        ],
     )(first_fields, second_fields, tiles)
 
 

time: 133 us -> 133 us (level)
  no operation moved by 1% of the time
where the time goes in v2:
time: 133 us
  Pallas kernels  132 us (99%)
    pallas_call x1, Pallas kernels, on_device(): pl.pallas_call(kernel, out_shape=(fields, fields, jax.ShapeDtypeStruct((T...  130 us

profile of v2, /device:TPU:1, one launch (start us, length us, event | category | flops | bytes accessed | tf_op | source)
XLA Modules:
  0.0 132.8 jit_solution(11156264071581453072)
XLA Ops:
  0.6 129.9 %shard_map.103 = (bf16[64,2048]{1,0:T(8,128)(2,1)}, bf16[64,2048]{1,0:T(8,128)(2,1)}, f32[4,256,128]{2,1,0:T(8,128)}, bf16[8,4096,128]{2,1,0:T(8,128)(2,1)}) custom-call(bf16[64,2048]{1,0:T(8,128)(2,1)} %noise1_hbm.1, bf16[64,2048]{1,0:T(8,128)(2,1)} %noise2_hbm.1, bf16[8,256,256]{2,1,0:T(8,128)(2,1)} %root1_hbm.1, bf16[8,256,256]{2,1,0:T(8,128)(2,1)} %root2_hbm.1, ...), custom_call_target="tpu_custom_call" | custom-call | flops 2300000000 | bytes 30000000 | tf_op jit(solution)/shard_map/pallas_call | solution.py:405
  130.5 2.3 %shard_map.104 = (bf16[64,2048]{1,0:T(8,128)(2,1)}, bf16[64,2048]{1,0:T(8,128)(2,1)}, f32[256,4,128]{2,1,0:T(4,128)}) custom-call(bf16[64,2048]{1,0:T(8,128)(2,1)} %get-tuple-element.6.first_in, bf16[64,2048]{1,0:T(8,128)(2,1)} %get-tuple-element.7.second_in, f32[4,256,128]{2,1,0:T(8,128)} %get-tuple-element.8.map_in), custom_call_target="tpu_custom_call" | custom-call | tf_op jit(solution)/shard_map/pallas_call | solution.py:443
